TPU v7x, 512 devices: a whole 4x4x16 slice. The times are simulated.
512 devices in a mesh: replica: 32 (over z, x_lo), fsdp: 16 (over y, x_hi, core).
Axes of the slice: x: 4 (x_hi: 2, x_lo: 2; x = x_hi * 2 + x_lo), y: 4, z: 16, core: 2. Of those that a mesh axis runs over, the one named last changes fastest.
Arguments:
- hidden: bfloat16 [32, 2048, 8192], P('replica', 'fsdp'), may hold values from -6 to 6
- norm_gain: float32 [8192], replicated, may hold values from 0.1 to 1.9
- dkeys: bfloat16 [32, 2048, 1024], P('replica', 'fsdp'), may hold values from -6 to 6
- local_weights: bfloat16 [32, 8192, 1024], P('replica', 'fsdp'), may hold values from -6 to 6
- outer_params: float32 [8192, 1024], P('fsdp', 'replica'), may hold values from -6 to 6
- momentum: float32 [8192, 1024], P('fsdp', 'replica'), may hold values from -3 to 3
- sync_step: int32 [1], replicated, may hold values from 0 to 15
Outputs:
- next_weights: bfloat16 [32, 8192, 1024], P('replica', 'fsdp')
- outer_next: float32 [8192, 1024], P('fsdp', 'replica')
- momentum_next: float32 [8192, 1024], P('fsdp', 'replica')
All inputs are finite; a program needn't handle non-finite values.
Results may differ from a plain program's by a relative error of at most 0.015.
Values may be sent and summed in bfloat16 or wider, within the bound.
A program may use at most 64 MiB of HBM per device.

v0:
```python
import jax
import jax.numpy as jnp
from jax import lax
from jax.sharding import PartitionSpec as P

D = 8192
WARMUP = 8


def outer_update(average, momentum_old, outer_old, rate):
    momentum_new = 0.9 * momentum_old + average
    outer_new = outer_old - rate * (average + 0.9 * momentum_new)
    return (outer_new, momentum_new)


def on_device(hidden, norm_gain, dkeys, local_weights, outer_params, momentum, sync_step):
    scale = 1.0 / D**0.5
    values = hidden[0].astype(jnp.float32)
    inverse = lax.rsqrt(jnp.mean(values * values, axis=-1, keepdims=True) + 1e-05)
    normed = (values * inverse * norm_gain).astype(jnp.bfloat16)
    columns = lax.all_to_all(normed, "fsdp", split_axis=1, concat_axis=0, tiled=True)
    weights = local_weights[0]
    grad = (
        lax.dot_general(
            columns,
            lax.all_gather(dkeys[0], "fsdp", axis=0, tiled=True),
            (((0,), (0,)), ((), ())),
            preferred_element_type=jnp.float32,
        )
        * scale
    )
    weights_f = weights.astype(jnp.float32)
    stepped = weights_f - 1.0 * grad
    workers = lax.axis_size("replica")
    rate = 0.7 * jnp.minimum(1.0, (sync_step[0].astype(jnp.float32) + 1.0) / WARMUP)
    total = lax.psum(weights_f.astype(jnp.bfloat16), "replica").astype(jnp.float32)
    outer_whole, momentum_whole = (
        lax.all_gather(outer_params, "replica", axis=1, tiled=True),
        lax.all_gather(momentum, "replica", axis=1, tiled=True),
    )
    average = outer_whole - total / workers
    whole_outer, momentum_all = outer_update(average, momentum_whole, outer_whole, rate)
    width = outer_params.shape[1]
    offset = lax.axis_index("replica") * width
    outer_next = lax.dynamic_slice_in_dim(whole_outer, offset, width, 1)
    momentum_next = lax.dynamic_slice_in_dim(momentum_all, offset, width, 1)
    merged = (0.5 * stepped + 0.5 * whole_outer).astype(jnp.bfloat16)
    return (merged[None], outer_next, momentum_next)


def solution(mesh):
    placed = (
        P("replica", "fsdp", None),
        P(),
        P("replica", "fsdp", None),
        P("replica", "fsdp", None),
        P("fsdp", "replica"),
        P("fsdp", "replica"),
        P(),
    )
    return jax.shard_map(
        on_device,
        mesh=mesh,
        in_specs=placed,
        out_specs=(P("replica", "fsdp", None), P("fsdp", "replica"), P("fsdp", "replica")),
        check_vma=False,
    )
```

profile of v0, /device:TPU:1, one launch (start us, length us, event | category | flops | bytes accessed | tf_op | source)
XLA Modules:
  0.0 636.8 jit_solution(3849860078078170950)
XLA Ops:
  7.2 0.0 all-gather.7.cloned.1.call-start
  7.2 0.7 all-gather.7.cloned.1.call-update
  7.9 0.0 all-gather.5.cloned.1.call-start
  7.9 0.7 all-gather.5.cloned.1.call-update
  8.6 0.0 all-reduce.2.cloned.1.call-start
  8.7 0.7 all-reduce.2.cloned.1.call-update
  9.4 0.0 all-gather.9.cloned.1.call-start
  9.4 0.5 all-gather.9.cloned.1.call-update
  10.0 0.0 copy-start.3
  10.0 3.2 copy.24
  13.2 0.0 copy-done.3
  13.2 1.1 multiply_reduce_fusion
  14.3 2.2 multiply_convert_fusion
  16.5 10.4 %all-to-all-start = ((bf16[128,16,512]{0,2,1:T(8,128)(2,1)}), bf16[128,16,512]{0,2,1:T(8,128)(2,1)S(1)}, u32[]{:S(2)}, u32[]{:S(2)}) async-start(bf16[128,16,512]{0,2,1:T(8,128)(2,1)} %multiply_convert_fusion), calls=%async_computation | async-start | bytes 4194304 | tf_op jit(solution)/shard_map/all_to_all | solution.py:21
  27.6 39.2 %all-to-all-done = bf16[128,16,512]{0,2,1:T(8,128)(2,1)S(1)} async-done(((bf16[128,16,512]{0,2,1:T(8,128)(2,1)}), bf16[128,16,512]{0,2,1:T(8,128)(2,1)S(1)}, u32[]{:S(2)}, u32[]{:S(2)}) %all-to-all-start) | async-done | bytes 2097184 | tf_op jit(solution)/shard_map/all_to_all | solution.py:21
  66.7 0.0 copy-start.1
  66.7 1.4 copy-done.1
  68.1 2.9 copy.25
  71.0 59.9 %all-gather.7.cloned.1.call-done = f32[512,1024]{0,1:T(8,128)} async-done(((f32[512,32]{0,1:T(8,128)}), f32[512,1024]{0,1:T(8,128)}) %all-gather.7.cloned.1.call-update) | async-done | bytes 2097168 | tf_op jit(solution)/shard_map/all_gather | solution.py:39
  130.9 2.9 copy.27
  133.8 129.0 %all-gather.5.cloned.1.call-done = f32[512,1024]{0,1:T(8,128)} async-done(((f32[512,32]{0,1:T(8,128)}), f32[512,1024]{0,1:T(8,128)}) %all-gather.5.cloned.1.call-update) | async-done | bytes 2097168 | tf_op jit(solution)/shard_map/all_gather | solution.py:38
  262.9 2.9 copy.28
  265.8 264.0 %all-reduce.2.cloned.1.call-done = bf16[512,1024]{1,0:T(8,128)(2,1)} async-done(((bf16[512,1024]{1,0:T(8,128)(2,1)}), bf16[512,1024]{1,0:T(8,128)(2,1)}) %all-reduce.2.cloned.1.call-update) | async-done | bytes 1048592 | tf_op jit(solution)/shard_map/psum | solution.py:36
  529.7 0.0 copy-start.2
  529.7 3.6 multiply_add_fusion
  533.3 0.0 copy-start
  533.4 1.3 copy-done
  534.7 0.9 constant_dynamic-slice_fusion
  535.6 1.7 copy.29
  537.3 0.7 copy.30
  538.0 85.9 %all-gather.9.cloned.1.call-done = bf16[1,2048,1024]{2,1,0:T(8,128)(2,1)} async-done(((bf16[1,128,1024]{2,1,0:T(8,128)(2,1)}), bf16[1,2048,1024]{2,1,0:T(8,128)(2,1)}) %all-gather.9.cloned.1.call-update) | async-done | bytes 4194320 | tf_op jit(solution)/shard_map/all_gather | solution.py:26
  623.9 0.0 copy-done.2
  623.9 6.3 fusion.4
  (2 shorter events, 0.0 us)
Async XLA Ops:
  7.2 123.7 %all-gather.7.cloned.1.call-start = ((), (), s32[]{:S(2)}) async-start(), calls=%async_computation.3 | async-start | bytes 2162688 | tf_op jit(solution)/shard_map/all_gather | solution.py:39
  7.9 255.0 %all-gather.5.cloned.1.call-start = ((), (), s32[]{:S(2)}) async-start(), calls=%async_computation.1 | async-start | bytes 2162688 | tf_op jit(solution)/shard_map/all_gather | solution.py:38
  8.6 521.1 %all-reduce.2.cloned.1.call-start = ((), (), s32[]{:S(2)}) async-start(), calls=%async_computation.2 | async-start | bytes 2097152 | tf_op jit(solution)/shard_map/psum | solution.py:36
  9.4 614.6 %all-gather.9.cloned.1.call-start = ((), (), s32[]{:S(2)}) async-start(), calls=%async_computation.4 | async-start | bytes 4456448 | tf_op jit(solution)/shard_map/all_gather | solution.py:26
  10.0 3.2 copy-start.3
  16.5 50.2 %all-to-all-start = ((bf16[128,16,512]{0,2,1:T(8,128)(2,1)}), bf16[128,16,512]{0,2,1:T(8,128)(2,1)S(1)}, u32[]{:S(2)}, u32[]{:S(2)}) async-start(bf16[128,16,512]{0,2,1:T(8,128)(2,1)} %multiply_convert_fusion), calls=%async_computation | async-start | bytes 4194304 | tf_op jit(solution)/shard_map/all_to_all | solution.py:21
  66.7 1.4 copy-start.1
  529.7 94.2 %copy-start.2 = (bf16[1,512,1024]{2,1,0:T(8,128)(2,1)S(1)}, bf16[1,512,1024]{2,1,0:T(8,128)(2,1)}, u32[]{:S(2)}) copy-start(bf16[1,512,1024]{2,1,0:T(8,128)(2,1)} %param.10) | copy-start | bytes 3145732
  533.3 1.3 copy-start
Sparse Core Ops, SparseCore 0:
  10.1 120.7 all-gather.6
  133.0 129.8 all-gather.4
  265.8 263.9 all-reduce.1
  533.5 90.4 all-gather.8
where the time goes:
time: 637 us
  waiting for transfers between devices  581 us (91%)
  local copies, waits for them, and re-layouts  18 us (3%)
  between operations  14.5 us (2%)
  starting transfers between devices  10.5 us (2%)
  other arithmetic  6.89 us (1%)
    psum x1, waiting for transfers between devices, on_device(): lax.psum(weights_f.astype(jnp.bfloat16), 'replica').astype(jnp.float32)  264 us
    all_gather x1, waiting for transfers between devices, on_device(): lax.all_gather(outer_params, 'replica', axis=1, tiled=True)  129 us
    all_gather x1, waiting for transfers between devices, on_device(): lax.all_gather(dkeys[0], 'fsdp', axis=0, tiled=True)  85.9 us
    all_gather x1, waiting for transfers between devices, on_device(): lax.all_gather(momentum, 'replica', axis=1, tiled=True)  59.9 us
    all_to_all x1, waiting for transfers between devices, on_device(): lax.all_to_all(normed, 'fsdp', split_axis=1, concat_axis=0, tiled=True)  39.2 us
  transfers between devices with their start and end apart: 5, of which 5 were waited for; matrix products, arithmetic and copies ran while one was open for 3% of the time, Pallas kernels for 0%

commit v1 on v0

v1 whole, which is shorter than its diff:
```python
import jax
import jax.numpy as jnp
from jax import lax
from jax.experimental import pallas as pl
from jax.experimental.pallas import tpu as pltpu
from jax.sharding import PartitionSpec as P

D = 8192
X = 1024
WARMUP = 8
WORKERS = 32
RING = 16
ROWS = 512
TOK = 128
COLS = X // RING
HALF = COLS // 2
MESH = pl.DeviceIdType.MESH
F32 = jnp.float32
BF16 = jnp.bfloat16

PEERS = [(dy, dx, dc) for dx in (1, 0) for dy in (2, 1, 3, 0) for dc in (0, 1) if (dy, dx, dc) != (0, 0, 0)]


def kernel(
    step, hid, gain, dk, w, outer, mom,
    merged, outer_new, mom_new,
    hid_v, gain_v, dk_v, w_v, outer_v, mom_v,
    inv_v, send_v, norm_v, keys_v, wt, down, up, tot, xs, xr, gathered, acc, out_v, on_v, mn_v,
    load_sem, store_sem, a2a_s, a2a_r, key_s, key_r, rs_s, rs_r, x_s, x_r, ag_s, ag_r,
):
    rep, fs = lax.axis_index("replica"), lax.axis_index("fsdp")
    z, xl = rep // 2, rep % 2
    y, xh, core = fs // 4, (fs // 2) % 2, fs % 2

    def fs_at(dy, dx, dc):
        return ((y + dy) % 4) * 4 + ((xh + dx) % 2) * 2 + (core + dc) % 2

    def ring(dz):
        return (z + dz + RING) % RING

    def in_group(dy, dx, dc):
        return (rep, fs_at(dy, dx, dc))

    z_next, z_prev = (ring(1) * 2 + xl, fs), (ring(-1) * 2 + xl, fs)
    partner = (z * 2 + 1 - xl, fs)

    barrier = pltpu.get_barrier_semaphore()
    others = [in_group(*d) for d in PEERS] + [z_next, z_prev, partner]
    for dev in others:
        pl.semaphore_signal(barrier, inc=1, device_id=dev, device_id_type=MESH)

    loads = [
        pltpu.make_async_copy(a, b, load_sem.at[i])
        for i, (a, b) in enumerate(
            [(w, w_v), (dk, dk_v), (hid, hid_v), (gain, gain_v), (outer, outer_v), (mom, mom_v)]
        )
    ]
    for cp in loads:
        cp.start()

    started = []

    def send(src, dst, ss, rs, dev):
        cp = pltpu.make_async_remote_copy(
            src_ref=src, dst_ref=dst, send_sem=ss, recv_sem=rs, device_id=dev, device_id_type=MESH
        )
        cp.start()
        started.append(cp)
        return cp

    loads[0].wait()

    @pl.loop(0, X // 128)
    def _(j):
        cols = pl.ds(pl.multiple_of(j * 128, 128), 128)
        wt[cols, :] = w_v[:, cols].T

    loads[1].wait()
    for j in range(X // 128):
        keys_v[fs, pl.ds(j * 128, 128), :] = dk_v[:, j * 128 : (j + 1) * 128].T

    pl.semaphore_wait(barrier, len(others))

    def chunk(dz):
        return pl.ds(pl.multiple_of(ring(dz) * COLS, COLS), COLS)

    def rs_down(s):
        if s == 0:
            src = wt.at[chunk(-8)]
        else:
            rs_copies[("d", s - 1)].wait_recv()
            down[s - 1] = (down[s - 1].astype(F32) + wt[chunk(s - 8), :].astype(F32)).astype(BF16)
            src = down.at[s - 1]
        rs_copies[("d", s)] = send(src, down.at[s], rs_s.at[s], rs_r.at[s], z_prev)

    def rs_up(s):
        if s == 0:
            src = wt.at[chunk(7)]
        else:
            rs_copies[("u", s - 1)].wait_recv()
            up[s - 1] = (up[s - 1].astype(F32) + wt[chunk(7 - s), :].astype(F32)).astype(BF16)
            src = up.at[s - 1]
        rs_copies[("u", s)] = send(src, up.at[s], rs_s.at[8 + s], rs_r.at[8 + s], z_next)

    rs_copies = {}

    def rs_step(s):
        rs_down(s)
        if s < 7:
            rs_up(s)

    n_key = [0]
    key_copies = {}

    def key_send(name, src_slot, rows, to):
        i = n_key[0]
        n_key[0] += 1
        part = keys_v.at[src_slot, rows]
        key_copies[name] = send(part, part, key_s.at[i], key_r.at[i], in_group(*to))

    whole, first, second = pl.ds(0, X), pl.ds(0, X // 2), pl.ds(X // 2, X // 2)

    def keys_own():
        key_send("x", fs, whole, (0, 1, 0))
        key_send("up0", fs, whole, (1, 0, 0))
        key_send("down0", fs, whole, (3, 0, 0))
        key_send("c00", fs, whole, (0, 0, 1))

    def keys_x():
        key_copies["x"].wait_recv()
        slot = fs_at(0, 1, 0)
        key_send("up1", slot, whole, (1, 0, 0))
        key_send("down1", slot, whole, (3, 0, 0))
        key_send("c01", slot, whole, (0, 0, 1))

    def keys_y(dx):
        key_copies["up%d" % dx].wait_recv()
        slot = fs_at(3, dx, 0)
        key_send("upup%d" % dx, slot, first, (1, 0, 0))
        key_send("c3%d" % dx, slot, whole, (0, 0, 1))
        key_copies["down%d" % dx].wait_recv()
        slot = fs_at(1, dx, 0)
        key_send("downdown%d" % dx, slot, second, (3, 0, 0))
        key_send("c1%d" % dx, slot, whole, (0, 0, 1))

    def keys_far(dx):
        key_copies["upup%d" % dx].wait_recv()
        key_copies["downdown%d" % dx].wait_recv()
        key_send("c2%d" % dx, fs_at(2, dx, 0), whole, (0, 0, 1))

    def keys_core():
        for dy in range(4):
            for dx in range(2):
                key_copies["c%d%d" % (dy, dx)].wait_recv()

    def statistics():
        loads[2].wait()
        loads[3].wait()

        @pl.loop(0, TOK // 16)
        def _(i):
            rows = pl.ds(pl.multiple_of(i * 16, 16), 16)
            total = jnp.zeros((16, 512), F32)
            for b in range(D // 512):
                v = hid_v[rows, b * 512 : (b + 1) * 512].astype(F32)
                total = total + v * v
            mean = jnp.sum(total, axis=-1, keepdims=True) * (1.0 / D)
            inv_v[rows, :] = jnp.broadcast_to(lax.rsqrt(mean + 1e-05), (16, 128))

    def normed(b, k):
        cols = pl.ds(pl.multiple_of(b * ROWS + k * 128, 128), 128)
        return (hid_v[:, cols].astype(F32) * inv_v[...] * gain_v[:, cols]).astype(BF16)

    a2a = []

    def a2a_send(i):
        b = fs_at(*PEERS[i])
        for k in range(ROWS // 128):
            send_v[b, :, k * 128 : (k + 1) * 128] = normed(b, k)
        a2a.append(send(send_v.at[b], norm_v.at[fs], a2a_s.at[i], a2a_r.at[i], in_group(*PEERS[i])))

    def own_block():
        for k in range(ROWS // 128):
            norm_v[fs, :, k * 128 : (k + 1) * 128] = normed(fs, k)

    def multiply(base, n, add):
        @pl.loop(0, 4)
        def _(i):
            rows = pl.ds(pl.multiple_of(i * (X // 4), X // 4), X // 4)
            left = jnp.concatenate([keys_v[base + q, rows, :] for q in range(n)], axis=1)
            right = norm_v[base : base + n].reshape(n * TOK, ROWS)
            part = jnp.dot(left, right, preferred_element_type=F32)
            acc[rows, :] = acc[rows, :] + part if add else part

    def update():
        rs_copies[("d", 7)].wait_recv()
        rs_copies[("u", 6)].wait_recv()
        tot[...] = wt[chunk(0), :].astype(F32) + down[7].astype(F32) + up[6].astype(F32)
        mine = pl.ds(pl.multiple_of(xl * HALF, HALF), HALF)
        theirs = pl.ds(pl.multiple_of((1 - xl) * HALF, HALF), HALF)
        xs[...] = tot[theirs, :]
        cp = send(xs, xr, x_s.at[0], x_r.at[0], partner)
        loads[4].wait()
        loads[5].wait()
        rate = 0.7 * jnp.minimum(1.0, (step[0].astype(F32) + 1.0) / WARMUP)
        cp.wait_recv()
        average = outer_v[...] - (tot[mine, :] + xr[...]) / WORKERS
        momentum = 0.9 * mom_v[...] + average
        new = outer_v[...] - rate * (average + 0.9 * momentum)
        mn_v[...] = momentum
        on_v[...] = new
        gathered[pl.ds(pl.multiple_of(z * COLS + xl * HALF, HALF), HALF), :] = new.astype(BF16)

    def piece(dz, other):
        half = 1 - xl if other else xl
        return pl.ds(pl.multiple_of(ring(dz) * COLS + half * HALF, HALF), HALF)

    ag = {}

    def ag_send(way, s, other):
        i = (way * 8 + s) * 2 + other
        part = gathered.at[piece(-s if way == 0 else s, other)]
        ag[(way, s, other)] = send(part, part, ag_s.at[i], ag_r.at[i], z_next if way == 0 else z_prev)

    def ag_step(s):
        for other in (0, 1):
            for way in (0, 1):
                if s > 0 and not (way == 1 and s > 7):
                    ag[(way, s - 1, other)].wait_recv()
                if s < (8, 7)[way]:
                    if s == 0 and other == 1 and way == 0:
                        x_ag.wait_recv()
                    ag_send(way, s, other)

    def finish(dm, n):
        m = (z // 2 + dm + 8) % 8
        rows = pl.ds(pl.multiple_of(m * 128, 128), 128)
        scale = 1.0 / D**0.5
        stepped = wt[rows, :].astype(F32) - 1.0 * (acc[rows, :] * scale)
        out_v[:, rows] = (0.5 * stepped + 0.5 * gathered[rows, :].astype(F32)).astype(BF16).T
        cp = pltpu.make_async_copy(out_v.at[:, rows], merged.at[:, rows], store_sem.at[n])
        cp.start()
        stores.append(cp)

    stores = []

    rs_step(0)
    keys_own()
    statistics()
    for i in range(0, 6):
        a2a_send(i)
    rs_step(1)
    for i in range(6, 15):
        a2a_send(i)
    own_block()
    rs_step(2)
    keys_x()
    rs_step(3)
    keys_y(0)
    rs_step(4)
    rs_step(5)
    keys_y(1)
    rs_step(6)
    rs_step(7)
    keys_far(0)
    update()
    x_ag = send(gathered.at[piece(0, 0)], gathered.at[piece(0, 0)], x_s.at[1], x_r.at[1], partner)
    ag_step(0)
    for i, (a, b) in enumerate([(on_v, outer_new), (mn_v, mom_new)]):
        cp = pltpu.make_async_copy(a, b, store_sem.at[8 + i])
        cp.start()
        stores.append(cp)
    keys_far(1)
    ag_step(1)
    ag_step(2)
    ag_step(3)
    keys_core()
    for cp in a2a:
        cp.wait_recv()
    ag_step(4)
    multiply(0, 8, False)
    ag_step(5)
    multiply(8, 8, True)
    ag_step(6)
    for n, dm in enumerate([0, 1, -1]):
        finish(dm, n)
    ag_step(7)
    for n, dm in enumerate([2, -2, 3, -3]):
        finish(dm, 3 + n)
    ag_step(8)
    finish(4, 7)
    for cp in stores:
        cp.wait()
    for cp in started:
        cp.wait_send()


def on_device(hidden, norm_gain, dkeys, local_weights, outer_params, momentum, sync_step):
    any_ = pl.BlockSpec(memory_space=pltpu.HBM)
    dma = pltpu.SemaphoreType.DMA
    merged, outer_new, mom_new = pl.pallas_call(
        kernel,
        out_shape=[
            jax.ShapeDtypeStruct((ROWS, X), BF16),
            jax.ShapeDtypeStruct((HALF, ROWS), F32),
            jax.ShapeDtypeStruct((HALF, ROWS), F32),
        ],
        in_specs=[pl.BlockSpec(memory_space=pltpu.SMEM)] + [any_] * 6,
        out_specs=[any_] * 3,
        scratch_shapes=[
            pltpu.VMEM((TOK, D), BF16),
            pltpu.VMEM((1, D), F32),
            pltpu.VMEM((TOK, X), BF16),
            pltpu.VMEM((ROWS, X), BF16),
            pltpu.VMEM((HALF, ROWS), F32),
            pltpu.VMEM((HALF, ROWS), F32),
            pltpu.VMEM((TOK, 128), F32),
            pltpu.VMEM((16, TOK, ROWS), BF16),
            pltpu.VMEM((16, TOK, ROWS), BF16),
            pltpu.VMEM((16, X, TOK), BF16),
            pltpu.VMEM((X, ROWS), BF16),
            pltpu.VMEM((8, COLS, ROWS), BF16),
            pltpu.VMEM((7, COLS, ROWS), BF16),
            pltpu.VMEM((COLS, ROWS), F32),
            pltpu.VMEM((HALF, ROWS), F32),
            pltpu.VMEM((HALF, ROWS), F32),
            pltpu.VMEM((X, ROWS), BF16),
            pltpu.VMEM((X, ROWS), F32),
            pltpu.VMEM((ROWS, X), BF16),
            pltpu.VMEM((HALF, ROWS), F32),
            pltpu.VMEM((HALF, ROWS), F32),
            dma((6,)), dma((10,)), dma((15,)), dma((15,)), dma((17,)), dma((17,)),
            dma((15,)), dma((15,)), dma((2,)), dma((2,)), dma((32,)), dma((32,)),
        ],
        compiler_params=pltpu.CompilerParams(
            collective_id=0, has_side_effects=True, vmem_limit_bytes=60 << 20
        ),
        name="outer_sync",
    )(
        sync_step, hidden[0], norm_gain.reshape(1, D), dkeys[0], local_weights[0],
        outer_params.T, momentum.T,
    )
    return merged[None], outer_new.T, mom_new.T


def solution(mesh):
    placed = (
        P("replica", "fsdp", None),
        P(),
        P("replica", "fsdp", None),
        P("replica", "fsdp", None),
        P("fsdp", "replica"),
        P("fsdp", "replica"),
        P(),
    )
    return jax.shard_map(
        on_device,
        mesh=mesh,
        in_specs=placed,
        out_specs=(P("replica", "fsdp", None), P("fsdp", "replica"), P("fsdp", "replica")),
        check_vma=False,
    )
```

time: 637 us -> 96.5 us (0.15)
  the two profiles are of different devices: /device:TPU:1 before, /device:TPU:2 now
where the time goes in v1:
time: 96.5 us; the launch traced here: 96.3 us
  Pallas kernels  91.5 us (95%)
  local copies, waits for them, and re-layouts  3.56 us (4%)
  between operations  1.31 us (1%)
    pallas_call x1, Pallas kernels, on_device(): pl.pallas_call(kernel, out_shape=[jax.ShapeDtypeStruct((ROWS, X), BF16),...  91.5 us
    unnamed x7, local copies, waits for them, and re-layouts  3.56 us

profile of v1, /device:TPU:2, one launch (start us, length us, event | category | flops | bytes accessed | tf_op | source)
XLA Modules:
  0.0 96.3 jit_solution(12201050387712219563)
XLA Ops:
  1.3 91.5 %outer_sync.1 = (bf16[512,1024]{1,0:T(8,128)(2,1)}, f32[32,512]{1,0:T(8,128)}, f32[32,512]{1,0:T(8,128)}) custom-call(s32[1]{0:T(128)S(6)} %copy.13.step, bf16[128,8192]{1,0:T(8,128)(2,1)} %bitcast.9, f32[1,8192]{1,0:T(1,128)} %bitcast.17, bf16[128,1024]{1,0:T(8,128)(2,1)} %bitcast.12, bf16[512,1024]{1,0:T(8,128)(2,1)} %bitcast.11, f32[32,512]{1,0:T(8,128)} %bitcast.15, ...), custom_call_target="tpu_custom_call" | custom-call | tf_op jit(solution)/shard_map/outer_sync/pallas_call | solution.py:301
  92.8 0.0 copy-start.1
  92.8 0.0 copy-start
  92.8 2.3 %copy.14 = bf16[1,512,1024]{2,1,0:T(8,128)(2,1)} copy(bf16[1,512,1024]{2,1,0:T(8,128)(2,1)} %bitcast.10) | data formatting | bytes 2097152
  95.1 0.0 copy-done.1
  95.1 0.6 copy.15
  95.7 0.0 copy-done
  95.7 0.6 copy.16
Async XLA Ops:
  92.8 2.3 %copy-start.1 = (f32[32,512]{1,0:T(8,128)S(1)}, f32[32,512]{1,0:T(8,128)}, u32[]{:S(2)}) copy-start(f32[32,512]{1,0:T(8,128)} %get-tuple-element.7) | copy-start | bytes 196612
  92.8 2.9 %copy-start = (f32[32,512]{1,0:T(8,128)S(1)}, f32[32,512]{1,0:T(8,128)}, u32[]{:S(2)}) copy-start(f32[32,512]{1,0:T(8,128)} %get-tuple-element.8) | copy-start | bytes 196612

commit v2 on v1

v2 whole, which is shorter than its diff:
```python
import jax
import jax.numpy as jnp
from jax import lax
from jax.experimental import pallas as pl
from jax.experimental.pallas import tpu as pltpu
from jax.sharding import PartitionSpec as P

D = 8192
X = 1024
WARMUP = 8
WORKERS = 32
RING = 16
ROWS = 512
TOK = 128
COLS = X // RING
HALF = COLS // 2
MESH = pl.DeviceIdType.MESH
F32 = jnp.float32
BF16 = jnp.bfloat16

SAME = [(dy, dx, 0) for dx in (1, 0) for dy in (2, 1, 3, 0) if (dy, dx) != (0, 0)]
CROSS = [(dy, dx, 1) for dx in (1, 0) for dy in (2, 1, 3, 0)]
PLACES = [p for pair in zip(SAME, CROSS) for p in pair] + CROSS[7:]
CHAINS = [(-1, (8, 6, 4, 2)), (-1, (7, 5, 3, 1)), (1, (7, 5, 3, 1)), (1, (6, 4, 2))]
AG_FAR = {1: 8, -1: 7}
PAIR_ORDER = [way * c[k] for k in range(4) for way, c in CHAINS if k < len(c)] + [0]


def kernel(
    step, hid, gain, dk, w, outer, mom,
    merged, outer_new, mom_new,
    hid_v, gain_v, dk_v, w_v, outer_v, mom_v,
    inv_v, send_v, norm_v, keys_v, wt, pair_v, first_v, chain_v, gathered, acc, out_v, on_v, mn_v,
    load_sem, store_sem, a2a_s, a2a_r, key_s, key_r, pair_s, pair_r, rs_s, rs_r, x_s, x_r, ag_s, ag_r,
):
    rep, fs = lax.axis_index("replica"), lax.axis_index("fsdp")
    z, xl = rep // 2, rep % 2
    y, xh, core = fs // 4, (fs // 2) % 2, fs % 2

    def ring(dz):
        return (z + dz + RING) % RING

    def in_group(dy, dx, dc):
        return (rep, ((y + dy) % 4) * 4 + ((xh + dx) % 2) * 2 + (core + dc) % 2)

    def on_ring(dz):
        return (ring(dz) * 2 + xl, fs)

    def slot(dy, dx, dc):
        return ((core + dc) % 2) * 8 + ((y + dy) % 4) * 2 + (xh + dx) % 2

    partner = (z * 2 + 1 - xl, fs)

    barrier = pltpu.get_barrier_semaphore()
    others = [in_group(*d) for d in SAME + CROSS] + [on_ring(d) for d in (1, -1, 2, -2)] + [partner]
    for dev in others:
        pl.semaphore_signal(barrier, inc=1, device_id=dev, device_id_type=MESH)

    loads = [
        pltpu.make_async_copy(a, b, load_sem.at[i])
        for i, (a, b) in enumerate(
            [(w, w_v), (dk, dk_v), (hid, hid_v), (gain, gain_v), (outer, outer_v), (mom, mom_v)]
        )
    ]
    for cp in loads:
        cp.start()

    started = []

    def send(src, dst, ss, rs, dev):
        cp = pltpu.make_async_remote_copy(
            src_ref=src, dst_ref=dst, send_sem=ss, recv_sem=rs, device_id=dev, device_id_type=MESH
        )
        cp.start()
        started.append(cp)
        return cp

    def turn_weights():
        loads[0].wait()

        @pl.loop(0, X // 128)
        def _(j):
            cols = pl.ds(pl.multiple_of(j * 128, 128), 128)
            wt[cols, :] = w_v[:, cols].T

    def turn_keys():
        loads[1].wait()
        for j in range(X // 128):
            keys_v[slot(0, 0, 0), pl.ds(j * 128, 128), :] = dk_v[:, j * 128 : (j + 1) * 128].T

    def owned(dz, half):
        return pl.ds(pl.multiple_of(ring(dz) * COLS + half * HALF, HALF), HALF)

    pairs = {}

    def pair_send(dz):
        i = len(pairs)
        pairs[dz] = send(wt.at[owned(dz, 1 - xl)], pair_v.at[ring(dz)], pair_s.at[i], pair_r.at[i], partner)

    def pair_sum(dz):
        pairs[dz].wait_recv()
        return wt[owned(dz, xl), :].astype(F32) + pair_v[ring(dz)].astype(F32)

    links = {}

    def rs_step(k):
        for n, (way, distances) in enumerate(CHAINS):
            if k >= len(distances):
                continue
            d = distances[k]
            i = n * 4 + k
            part = pair_sum(way * d)
            if k == 0:
                src, at = first_v.at[n], (first_v, n)
            else:
                links[(n, k - 1)].wait_recv()
                src, at = chain_v.at[i - 1], (chain_v, i - 1)
                part = part + chain_v[i - 1].astype(F32)
            at[0][at[1]] = part.astype(BF16)
            links[(n, k)] = send(src, chain_v.at[i], rs_s.at[i], rs_r.at[i], on_ring(way * min(d, 2)))

    def update():
        total = pair_sum(0)
        for n, (_, distances) in enumerate(CHAINS):
            k = len(distances) - 1
            links[(n, k)].wait_recv()
            total = total + chain_v[n * 4 + k].astype(F32)
        loads[4].wait()
        loads[5].wait()
        rate = 0.7 * jnp.minimum(1.0, (step[0].astype(F32) + 1.0) / WARMUP)
        average = outer_v[...] - total / WORKERS
        momentum = 0.9 * mom_v[...] + average
        new = outer_v[...] - rate * (average + 0.9 * momentum)
        mn_v[...] = momentum
        on_v[...] = new
        gathered[owned(0, xl), :] = new.astype(BF16)

    ag, crossed = {}, {}

    def ag_send(way, d):
        hop = 1 if d == -1 else 2
        far = max(d, 0) + hop
        i = (far - 1) * 2 + (way + 1) // 2
        part = gathered.at[owned(-way * max(d, 0), xl)]
        ag[(way, far)] = send(part, part, ag_s.at[i], ag_r.at[i], on_ring(way * hop))

    def cross(way, d):
        i = d * 2 + (way + 1) // 2
        part = gathered.at[owned(-way * d, xl)]
        crossed[(way, d)] = send(part, part, x_s.at[i], x_r.at[i], partner)

    def ag_start():
        for d in (-1, 0):
            for way in (1, -1):
                ag_send(way, d)
        cross(1, 0)

    def ag_step(k):
        for d in (2 * k + 1, 2 * k + 2):
            for way in (1, -1):
                if d <= AG_FAR[way]:
                    ag[(way, d)].wait_recv()
                    if d + 2 <= AG_FAR[way]:
                        ag_send(way, d)
                    cross(way, d)

    def ag_crossed():
        for cp in crossed.values():
            cp.wait_recv()

    key_copies = {}

    def key_send(name, place, rows, to):
        i = len(key_copies)
        part = keys_v.at[slot(*place), rows]
        key_copies[name] = send(part, part, key_s.at[i], key_r.at[i], in_group(*to))

    whole, first, second = pl.ds(0, X), pl.ds(0, X // 2), pl.ds(X // 2, X // 2)

    def keys_own():
        key_send("x", (0, 0, 0), whole, (0, 1, 0))
        key_send("up0", (0, 0, 0), whole, (1, 0, 0))
        key_send("down0", (0, 0, 0), whole, (3, 0, 0))

    def keys_x():
        key_copies["x"].wait_recv()
        key_send("up1", (0, 1, 0), whole, (1, 0, 0))
        key_send("down1", (0, 1, 0), whole, (3, 0, 0))
        key_send("c01", (0, 1, 0), whole, (0, 0, 1))

    def keys_y(dx):
        key_copies["up%d" % dx].wait_recv()
        key_send("upup%d" % dx, (3, dx, 0), first, (1, 0, 0))
        key_send("c3%d" % dx, (3, dx, 0), whole, (0, 0, 1))
        key_copies["down%d" % dx].wait_recv()
        key_send("downdown%d" % dx, (1, dx, 0), second, (3, 0, 0))
        key_send("c1%d" % dx, (1, dx, 0), whole, (0, 0, 1))

    def keys_far(dx):
        key_copies["upup%d" % dx].wait_recv()
        key_copies["downdown%d" % dx].wait_recv()
        key_send("c2%d" % dx, (2, dx, 0), whole, (0, 0, 1))

    def statistics():
        loads[2].wait()
        loads[3].wait()

        @pl.loop(0, TOK // 16)
        def _(i):
            rows = pl.ds(pl.multiple_of(i * 16, 16), 16)
            total = jnp.zeros((16, 512), F32)
            for b in range(D // 512):
                v = hid_v[rows, b * 512 : (b + 1) * 512].astype(F32)
                total = total + v * v
            mean = jnp.sum(total, axis=-1, keepdims=True) * (1.0 / D)
            inv_v[rows, :] = jnp.broadcast_to(lax.rsqrt(mean + 1e-05), (16, 128))

    def normed(b, k):
        cols = pl.ds(pl.multiple_of(b * ROWS + k * 128, 128), 128)
        return (hid_v[:, cols].astype(F32) * inv_v[...] * gain_v[:, cols]).astype(BF16)

    a2a = {}

    def a2a_send(place):
        i = len(a2a)
        dev = in_group(*place)
        for k in range(ROWS // 128):
            send_v[i, :, k * 128 : (k + 1) * 128] = normed(dev[1], k)
        a2a[place] = send(send_v.at[i], norm_v.at[slot(0, 0, 0)], a2a_s.at[i], a2a_r.at[i], dev)

    def own_block():
        for k in range(ROWS // 128):
            norm_v[slot(0, 0, 0), :, k * 128 : (k + 1) * 128] = normed(fs, k)

    def multiply(dc):
        base = ((core + dc) % 2) * 8

        @pl.loop(0, 4)
        def _(i):
            rows = pl.ds(pl.multiple_of(i * (X // 4), X // 4), X // 4)
            left = jnp.concatenate([keys_v[base + q, rows, :] for q in range(8)], axis=1)
            right = norm_v[pl.ds(base, 8)].reshape(8 * TOK, ROWS)
            part = jnp.dot(left, right, preferred_element_type=F32)
            acc[rows, :] = acc[rows, :] + part if dc else part

    def grad_same():
        for place in SAME:
            a2a[place].wait_recv()
        multiply(0)

    def grad_cross():
        for place in CROSS:
            a2a[place].wait_recv()
        for dy in range(4):
            for dx in range(2):
                key_copies["c%d%d" % (dy, dx)].wait_recv()
        multiply(1)

    stores = []

    def store(src, dst):
        cp = pltpu.make_async_copy(src, dst, store_sem.at[len(stores)])
        cp.start()
        stores.append(cp)

    def finish(dm):
        m = (z // 2 + dm + 8) % 8
        rows = pl.ds(pl.multiple_of(m * 128, 128), 128)
        scale = 1.0 / D**0.5
        stepped = wt[rows, :].astype(F32) - 1.0 * (acc[rows, :] * scale)
        out_v[:, rows] = (0.5 * stepped + 0.5 * gathered[rows, :].astype(F32)).astype(BF16).T
        store(out_v.at[:, rows], merged.at[:, rows])

    turn_weights()
    pl.semaphore_wait(barrier, len(others))
    for dz in PAIR_ORDER:
        pair_send(dz)
    turn_keys()
    keys_own()
    key_send("c00", (0, 0, 0), whole, (0, 0, 1))
    statistics()
    for place in PLACES[:6]:
        a2a_send(place)
    rs_step(0)
    for place in PLACES[6:11]:
        a2a_send(place)
    rs_step(1)
    for place in PLACES[11:]:
        a2a_send(place)
    own_block()
    rs_step(2)
    keys_x()
    rs_step(3)
    keys_y(0)
    update()
    ag_start()
    store(on_v, outer_new)
    store(mn_v, mom_new)
    keys_y(1)
    ag_step(0)
    keys_far(0)
    ag_step(1)
    keys_far(1)
    ag_step(2)
    ag_step(3)
    grad_same()
    grad_cross()
    ag_crossed()
    for dm in (0, 1, -1, 2, -2, 3, -3, 4):
        finish(dm)
    for cp in stores:
        cp.wait()
    for cp in started:
        cp.wait_send()


def copy_kernel(merged, outer_new, mom_new, merged_out, outer_out, mom_out, merged_v, outer_v, mom_v, in_sem, out_sem):
    routes = [(merged.at[r], merged_v.at[r], merged_out.at[r]) for r in (pl.ds(128 * i, 128) for i in range(4))]
    routes += [(outer_new, outer_v, outer_out), (mom_new, mom_v, mom_out)]
    arrive = [pltpu.make_async_copy(a, b, in_sem.at[i]) for i, (a, b, _) in enumerate(routes)]
    leave = [pltpu.make_async_copy(b, c, out_sem.at[i]) for i, (_, b, c) in enumerate(routes)]
    for cp in arrive:
        cp.start()
    for a, b in zip(arrive, leave):
        a.wait()
        b.start()
    for cp in leave:
        cp.wait()


def on_device(hidden, norm_gain, dkeys, local_weights, outer_params, momentum, sync_step):
    any_ = pl.BlockSpec(memory_space=pltpu.HBM)
    dma = pltpu.SemaphoreType.DMA
    merged, outer_new, mom_new = pl.pallas_call(
        kernel,
        out_shape=[
            jax.ShapeDtypeStruct((ROWS, X), BF16),
            jax.ShapeDtypeStruct((HALF, ROWS), F32),
            jax.ShapeDtypeStruct((HALF, ROWS), F32),
        ],
        in_specs=[pl.BlockSpec(memory_space=pltpu.SMEM)] + [any_] * 6,
        out_specs=[any_] * 3,
        scratch_shapes=[
            pltpu.VMEM((TOK, D), BF16),
            pltpu.VMEM((1, D), F32),
            pltpu.VMEM((TOK, X), BF16),
            pltpu.VMEM((ROWS, X), BF16),
            pltpu.VMEM((HALF, ROWS), F32),
            pltpu.VMEM((HALF, ROWS), F32),
            pltpu.VMEM((TOK, 128), F32),
            pltpu.VMEM((16, TOK, ROWS), BF16),
            pltpu.VMEM((16, TOK, ROWS), BF16),
            pltpu.VMEM((16, X, TOK), BF16),
            pltpu.VMEM((X, ROWS), BF16),
            pltpu.VMEM((RING, HALF, ROWS), BF16),
            pltpu.VMEM((4, HALF, ROWS), BF16),
            pltpu.VMEM((15, HALF, ROWS), BF16),
            pltpu.VMEM((X, ROWS), BF16),
            pltpu.VMEM((X, ROWS), F32),
            pltpu.VMEM((ROWS, X), BF16),
            pltpu.VMEM((HALF, ROWS), F32),
            pltpu.VMEM((HALF, ROWS), F32),
            dma((6,)), dma((10,)), dma((15,)), dma((15,)), dma((17,)), dma((17,)), dma((16,)), dma((16,)),
            dma((15,)), dma((15,)), dma((18,)), dma((18,)), dma((16,)), dma((16,)),
        ],
        compiler_params=pltpu.CompilerParams(
            collective_id=0, has_side_effects=True, vmem_limit_bytes=60 << 20
        ),
        name="outer_sync",
    )(
        sync_step, hidden[0], norm_gain.reshape(1, D), dkeys[0], local_weights[0],
        outer_params.T, momentum.T,
    )
    results = [merged, outer_new, mom_new]
    merged, outer_new, mom_new = pl.pallas_call(
        copy_kernel,
        out_shape=[jax.ShapeDtypeStruct(a.shape, a.dtype) for a in results],
        in_specs=[any_] * 3,
        out_specs=[any_] * 3,
        scratch_shapes=[pltpu.VMEM(a.shape, a.dtype) for a in results] + [dma((6,)), dma((6,))],
        compiler_params=pltpu.CompilerParams(vmem_limit_bytes=60 << 20),
        name="results",
    )(*results)
    return merged[None], outer_new.T, mom_new.T


def solution(mesh):
    placed = (
        P("replica", "fsdp", None),
        P(),
        P("replica", "fsdp", None),
        P("replica", "fsdp", None),
        P("fsdp", "replica"),
        P("fsdp", "replica"),
        P(),
    )
    return jax.shard_map(
        on_device,
        mesh=mesh,
        in_specs=placed,
        out_specs=(P("replica", "fsdp", None), P("fsdp", "replica"), P("fsdp", "replica")),
        check_vma=False,
    )
```

time: 96.5 us -> 75.7 us (0.78)
  the two profiles are of different devices: /device:TPU:2 before, /device:TPU:4 now
where the time goes in v2:
time: 75.7 us; the launch traced here: 75.6 us
  Pallas kernels  74.3 us (98%)
  between operations  1.29 us (2%)
    pallas_call x1, Pallas kernels, on_device(): pl.pallas_call(kernel, out_shape=[jax.ShapeDtypeStruct((ROWS, X), BF16),...  72.2 us
    pallas_call x1, Pallas kernels, on_device(): pl.pallas_call(copy_kernel, out_shape=[jax.ShapeDtypeStruct(a.shape, a.dt...  2.05 us

profile of v2, /device:TPU:4, one launch (start us, length us, event | category | flops | bytes accessed | tf_op | source)
XLA Modules:
  0.0 75.6 jit_solution(15966988946246878549)
XLA Ops:
  1.3 72.2 %outer_sync.1 = (bf16[512,1024]{1,0:T(8,128)(2,1)}, f32[32,512]{1,0:T(8,128)}, f32[32,512]{1,0:T(8,128)}) custom-call(s32[1]{0:T(128)S(6)} %copy.10.step, bf16[128,8192]{1,0:T(8,128)(2,1)} %bitcast.9, f32[1,8192]{1,0:T(1,128)} %bitcast.14, bf16[128,1024]{1,0:T(8,128)(2,1)} %bitcast.11, bf16[512,1024]{1,0:T(8,128)(2,1)} %bitcast.10, f32[32,512]{1,0:T(8,128)} %bitcast.12, ...), custom_call_target="tpu_custom_call" | custom-call | tf_op jit(solution)/shard_map/outer_sync/pallas_call | solution.py:334
  73.5 2.1 %results.1 = (bf16[512,1024]{1,0:T(8,128)(2,1)}, f32[32,512]{1,0:T(8,128)}, f32[32,512]{1,0:T(8,128)}) custom-call(bf16[512,1024]{1,0:T(8,128)(2,1)} %get-tuple-element.9.merged, f32[32,512]{1,0:T(8,128)} %get-tuple-element.10.outer_new, f32[32,512]{1,0:T(8,128)} %get-tuple-element.11.mom_new), custom_call_target="tpu_custom_call" | custom-call | tf_op jit(solution)/shard_map/results/pallas_call | solution.py:375

commit v3 on v2

v3 whole, which is shorter than its diff:
```python
import jax
import jax.numpy as jnp
from jax import lax
from jax.experimental import pallas as pl
from jax.experimental.pallas import tpu as pltpu
from jax.sharding import PartitionSpec as P

D = 8192
X = 1024
WARMUP = 8
WORKERS = 32
RING = 16
ROWS = 512
TOK = 128
COLS = X // RING
HALF = COLS // 2
MESH = pl.DeviceIdType.MESH
F32 = jnp.float32
BF16 = jnp.bfloat16

PLACES = [(dy, dx, dc) for dx in (0, 1) for dy in (2, 1, 3, 0) for dc in (0, 1) if (dy, dx, dc) != (0, 0, 0)]
CHAINS = [(-1, (8, 6, 4, 2)), (-1, (7, 5, 3, 1)), (1, (7, 5, 3, 1)), (1, (6, 4, 2))]
AG_FAR = {1: 8, -1: 7}
PAIR_ORDER = [way * c[k] for k in range(4) for way, c in CHAINS if k < len(c)] + [0]
KEYS = ["own", "x"] + [n + d for d in "01" for n in ("up", "down", "upup", "downdown", "s3", "s1", "s2")] + ["s01"]


def kernel(
    step, hid, gain, dk, w, outer, mom,
    merged, outer_new, mom_new,
    hid_v, gain_v, dk_v, w_v, outer_v, mom_v,
    inv_v, send_v, norm_v, keys_v, wt, other_wt, pair_v, first_v, chain_v, gathered, acc, out_v, on_v, mn_v,
    load_sem, store_sem, a2a_s, a2a_r, key_s, key_r, pair_s, pair_r, core_s, core_r,
    rs_s, rs_r, ag_s, ag_r, x_s, x_r, c_s, c_r, go_sem,
):
    rep, fs = lax.axis_index("replica"), lax.axis_index("fsdp")
    z, xl = rep // 2, rep % 2
    y, xh, core = fs // 4, (fs // 2) % 2, fs % 2

    def ring(dz):
        return (z + dz + RING) % RING

    def in_group(dy, dx, dc):
        return (rep, ((y + dy) % 4) * 4 + ((xh + dx) % 2) * 2 + (core + dc) % 2)

    def on_ring(dz):
        return (ring(dz) * 2 + xl, fs)

    def chip(dy, dx):
        return ((xh + dx) % 2) * 4 + (y + dy) % 4

    sibling = (rep, fs + 1 - 2 * core)
    partner = (z * 2 + 1 - xl, fs)
    across = (z * 2 + 1 - xl, fs + 1 - 2 * core)

    barrier = pltpu.get_barrier_semaphore()
    group = [(rep, (fs // 2 + i) % 8 * 2) for i in range(8)] + [(partner[0], fs - core)]
    along = [on_ring(d) for d in (1, -1, 2, -2)]

    def greet(dev):
        pl.semaphore_signal(barrier, inc=1, device_id=dev, device_id_type=MESH)

    for dev in group[1:]:
        greet(dev)

    @pl.when(core == 1)
    def _():
        greet(group[0])
        for dev in along:
            greet(dev)

    def group_is_in():
        @pl.when(core == 0)
        def _():
            pl.semaphore_wait(barrier, 17)
            pl.semaphore_signal(go_sem, inc=1, device_id=sibling, device_id_type=MESH)

        @pl.when(core == 1)
        def _():
            pl.semaphore_wait(go_sem, 1)

    def neighbours_are_in():
        pl.semaphore_wait(barrier, len(along))

    loads = [
        pltpu.make_async_copy(a, b, load_sem.at[i])
        for i, (a, b) in enumerate(
            [
                (w, w_v), (dk, dk_v), (hid, hid_v), (gain, gain_v),
                (outer, outer_v.at[core]), (mom, mom_v.at[core]),
            ]
        )
    ]
    for cp in loads:
        cp.start()

    loads[0].wait()

    @pl.loop(0, X // 128)
    def _(j):
        cols = pl.ds(pl.multiple_of(j * 128, 128), 128)
        wt[pl.ds(2 * j, 2)] = w_v[:, cols].T.reshape(2, 2, HALF, ROWS)

    loads[1].wait()
    for j in range(X // 128):
        keys_v[chip(0, 0), core, pl.ds(j * 128, 128), :] = dk_v[:, j * 128 : (j + 1) * 128].T

    for cp in loads[2:]:
        cp.wait()

    group_is_in()

    started = []

    def send(src, dst, ss, rs, dev):
        cp = pltpu.make_async_remote_copy(
            src_ref=src, dst_ref=dst, send_sem=ss, recv_sem=rs, device_id=dev, device_id_type=MESH
        )
        cp.start()
        started.append(cp)

    def arrive(dst, rs):
        pltpu.make_async_remote_copy(
            src_ref=dst, dst_ref=dst, send_sem=rs, recv_sem=rs, device_id=sibling, device_id_type=MESH
        ).wait_recv()

    def pair_send(to):
        for i, dz in enumerate(PAIR_ORDER):
            t = ring(dz)
            send(wt.at[t, 1 - xl], pair_v.at[core, t], pair_s.at[i], pair_r.at[core, i], to)

    def pair_sum(dz):
        t, i = ring(dz), PAIR_ORDER.index(dz)
        for c in (0, 1):
            arrive(pair_v.at[c, t], pair_r.at[c, i])
        return [
            other_wt[t].astype(F32) + pair_v[0, t].astype(F32),
            wt[t, xl].astype(F32) + pair_v[1, t].astype(F32),
        ]

    def rs_step(k):
        for n, (way, distances) in enumerate(CHAINS):
            if k >= len(distances):
                continue
            d = distances[k]
            i = n * 4 + k
            parts = pair_sum(way * d)
            if k == 0:
                buffer, at = first_v, n
            else:
                buffer, at = chain_v, i - 1
                arrive(chain_v.at[i - 1], rs_r.at[i - 1])
            for c in (0, 1):
                part = parts[c] if k == 0 else parts[c] + chain_v[i - 1, c].astype(F32)
                buffer[at, c] = part.astype(BF16)
            send(buffer.at[at], chain_v.at[i], rs_s.at[i], rs_r.at[i], on_ring(way * min(d, 2)))

    def update():
        totals = pair_sum(0)
        for n, (_, distances) in enumerate(CHAINS):
            i = n * 4 + len(distances) - 1
            arrive(chain_v.at[i], rs_r.at[i])
            totals = [totals[c] + chain_v[i, c].astype(F32) for c in (0, 1)]
        rate = 0.7 * jnp.minimum(1.0, (step[0].astype(F32) + 1.0) / WARMUP)
        arrive(outer_v.at[0], core_r.at[1])
        arrive(mom_v.at[0], core_r.at[2])
        for c in (0, 1):
            average = outer_v[c] - totals[c] / WORKERS
            momentum = 0.9 * mom_v[c] + average
            new = outer_v[c] - rate * (average + 0.9 * momentum)
            mn_v[c] = momentum
            on_v[c] = new
            gathered[z, xl, c] = new.astype(BF16)

    def ag_send(way, d):
        hop = 1 if d == -1 else 2
        far = max(d, 0) + hop
        i = (far - 1) * 2 + (way + 1) // 2
        part = gathered.at[ring(-way * max(d, 0)), xl]
        send(part, part, ag_s.at[i], ag_r.at[i], on_ring(way * hop))

    def cross(way, d):
        i = d * 2 + (way + 1) // 2 - 1
        t = ring(-way * d)
        for c, to in ((1, partner), (0, across)):
            part = gathered.at[t, xl, c]
            send(part, part, x_s.at[c, i], x_r.at[i], to)
        part = gathered.at[t, xl, 0]
        send(part, part, c_s.at[i], c_r.at[i], sibling)

    def ag_start():
        for d in (-1, 0):
            for way in (1, -1):
                ag_send(way, d)
        cross(1, 0)

    def ag_step(k):
        for d in (2 * k + 1, 2 * k + 2):
            for way in (1, -1):
                if d <= AG_FAR[way]:
                    i = (d - 1) * 2 + (way + 1) // 2
                    arrive(gathered.at[ring(-way * d), xl], ag_r.at[i])
                    if d + 2 <= AG_FAR[way]:
                        ag_send(way, d)
                    cross(way, d)

    def ag_crossed():
        for d in range(9):
            for way in (1, -1):
                if d <= AG_FAR[way] and (d, way) != (0, -1):
                    i, t = d * 2 + (way + 1) // 2 - 1, ring(-way * d)
                    arrive(gathered.at[t, 1 - xl, core], x_r.at[i])

    def ag_other_core():
        for d in range(9):
            for way in (1, -1):
                if d <= AG_FAR[way] and (d, way) != (0, -1):
                    i, t = d * 2 + (way + 1) // 2 - 1, ring(-way * d)
                    arrive(gathered.at[t, xl, 0], c_r.at[i])

    def key_send(name, part, to):
        i = KEYS.index(name)
        send(part, part, key_s.at[i], key_r.at[i], to)

    def key_arrive(name, part):
        arrive(part, key_r.at[KEYS.index(name)])

    def block(dy, dx):
        return keys_v.at[chip(dy, dx)]

    def keys_own():
        key_send("own", keys_v.at[chip(0, 0), core], sibling)

    def keys_start():
        key_arrive("own", keys_v.at[chip(0, 0), 1])
        key_send("up0", block(0, 0), in_group(1, 0, 0))
        key_send("down0", block(0, 0), in_group(3, 0, 0))
        key_send("x", block(0, 0), in_group(0, 1, 0))

    def keys_x():
        key_arrive("x", block(0, 1))
        key_send("up1", block(0, 1), in_group(1, 0, 0))
        key_send("down1", block(0, 1), in_group(3, 0, 0))
        key_send("s01", block(0, 1), sibling)

    def keys_y(dx):
        n = str(dx)
        key_arrive("up" + n, block(3, dx))
        key_send("upup" + n, keys_v.at[chip(3, dx), 0], in_group(1, 0, 0))
        key_send("s3" + n, block(3, dx), sibling)
        key_arrive("down" + n, block(1, dx))
        key_send("downdown" + n, keys_v.at[chip(1, dx), 1], in_group(3, 0, 0))
        key_send("s1" + n, block(1, dx), sibling)

    def keys_far(dx):
        n = str(dx)
        key_arrive("upup" + n, keys_v.at[chip(2, dx), 0])
        key_arrive("downdown" + n, keys_v.at[chip(2, dx), 1])
        key_send("s2" + n, block(2, dx), sibling)

    def keys_other_core(dx):
        for dy in (0, 1, 3, 2):
            if (dy, dx) != (0, 0):
                key_arrive("s%d%d" % (dy, dx), block(dy, dx))

    def statistics():
        @pl.loop(0, TOK // 16)
        def _(i):
            rows = pl.ds(pl.multiple_of(i * 16, 16), 16)
            total = jnp.zeros((16, 512), F32)
            for b in range(D // 512):
                v = hid_v[rows, b * 512 : (b + 1) * 512].astype(F32)
                total = total + v * v
            mean = jnp.sum(total, axis=-1, keepdims=True) * (1.0 / D)
            inv_v[rows, :] = jnp.broadcast_to(lax.rsqrt(mean + 1e-05), (16, 128))

    def normed(b, k):
        cols = pl.ds(pl.multiple_of(b * ROWS + k * 128, 128), 128)
        return (hid_v[:, cols].astype(F32) * inv_v[...] * gain_v[:, cols]).astype(BF16)

    def a2a_send(first, last):
        for i in range(first, last):
            dev = in_group(*PLACES[i])
            for k in range(ROWS // 128):
                send_v[i, :, k * 128 : (k + 1) * 128] = normed(dev[1], k)
            send(send_v.at[i], norm_v.at[chip(0, 0), core], a2a_s.at[i], a2a_r.at[i], dev)

    def own_block():
        for k in range(ROWS // 128):
            norm_v[chip(0, 0), core, :, k * 128 : (k + 1) * 128] = normed(fs, k)

    def multiply(dx):
        for i, (dy, px, dc) in enumerate(PLACES):
            if px == dx:
                arrive(norm_v.at[chip(-dy + 4, dx), (core + dc) % 2], a2a_r.at[i])
        base = ((xh + dx) % 2) * 4

        @pl.loop(0, 4)
        def _(i):
            rows = pl.ds(pl.multiple_of(i * (X // 4), X // 4), X // 4)
            left = jnp.concatenate([keys_v[base + q, c, rows, :] for q in range(4) for c in range(2)], axis=1)
            right = norm_v[pl.ds(base, 4)].reshape(8 * TOK, ROWS)
            part = jnp.dot(left, right, preferred_element_type=F32)
            acc[rows, :] = acc[rows, :] + part if dx else part

    stores = []

    def store(src, dst):
        cp = pltpu.make_async_copy(src, dst, store_sem.at[len(stores)])
        cp.start()
        stores.append(cp)

    def finish():
        scale = 1.0 / D**0.5
        for m in range(8):
            rows = pl.ds(m * 128, 128)
            old = wt[2 * m : 2 * m + 2].reshape(128, ROWS).astype(F32)
            new = gathered[2 * m : 2 * m + 2, :, core].reshape(128, ROWS).astype(F32)
            stepped = old - 1.0 * (acc[rows, :] * scale)
            out_v[:, m * 128 : (m + 1) * 128] = (0.5 * stepped + 0.5 * new).astype(BF16).T
            store(out_v.at[:, rows], merged.at[:, rows])

    def drain():
        for cp in stores:
            cp.wait()
        for cp in started:
            cp.wait_send()
        stores.clear()
        started.clear()

    @pl.when(core == 0)
    def _():
        send(wt.at[:, xl], other_wt, core_s.at[0], core_r.at[0], sibling)
        pair_send(across)
        keys_own()
        send(outer_v.at[0], outer_v.at[0], core_s.at[1], core_r.at[1], sibling)
        send(mom_v.at[0], mom_v.at[0], core_s.at[2], core_r.at[2], sibling)
        keys_start()
        statistics()
        a2a_send(0, 7)
        keys_x()
        a2a_send(7, 9)
        keys_y(0)
        a2a_send(9, 15)
        own_block()
        keys_y(1)
        keys_far(0)
        multiply(0)
        keys_far(1)
        multiply(1)
        arrive(on_v.at[0], core_r.at[3])
        arrive(mn_v.at[0], core_r.at[4])
        store(on_v.at[0], outer_new)
        store(mn_v.at[0], mom_new)
        ag_other_core()
        ag_crossed()
        finish()
        drain()

    @pl.when(core == 1)
    def _():
        pair_send(partner)
        keys_own()
        statistics()
        a2a_send(0, 4)
        arrive(other_wt, core_r.at[0])
        neighbours_are_in()
        rs_step(0)
        a2a_send(4, 10)
        rs_step(1)
        a2a_send(10, 15)
        own_block()
        rs_step(2)
        rs_step(3)
        update()
        ag_start()
        send(on_v.at[0], on_v.at[0], core_s.at[3], core_r.at[3], sibling)
        send(mn_v.at[0], mn_v.at[0], core_s.at[4], core_r.at[4], sibling)
        store(on_v.at[1], outer_new)
        store(mn_v.at[1], mom_new)
        for k in range(3):
            ag_step(k)
        key_arrive("own", keys_v.at[chip(0, 0), 0])
        keys_other_core(0)
        multiply(0)
        ag_step(3)
        keys_other_core(1)
        multiply(1)
        ag_crossed()
        finish()
        drain()


def copy_kernel(merged, outer_new, mom_new, merged_out, outer_out, mom_out, merged_v, outer_v, mom_v, in_sem, out_sem):
    routes = [(merged.at[r], merged_v.at[r], merged_out.at[r]) for r in (pl.ds(128 * i, 128) for i in range(4))]
    routes += [(outer_new, outer_v, outer_out), (mom_new, mom_v, mom_out)]
    arrive = [pltpu.make_async_copy(a, b, in_sem.at[i]) for i, (a, b, _) in enumerate(routes)]
    leave = [pltpu.make_async_copy(b, c, out_sem.at[i]) for i, (_, b, c) in enumerate(routes)]
    for cp in arrive:
        cp.start()
    for a, b in zip(arrive, leave):
        a.wait()
        b.start()
    for cp in leave:
        cp.wait()


def on_device(hidden, norm_gain, dkeys, local_weights, outer_params, momentum, sync_step):
    any_ = pl.BlockSpec(memory_space=pltpu.HBM)
    dma = pltpu.SemaphoreType.DMA
    merged, outer_new, mom_new = pl.pallas_call(
        kernel,
        out_shape=[
            jax.ShapeDtypeStruct((ROWS, X), BF16),
            jax.ShapeDtypeStruct((HALF, ROWS), F32),
            jax.ShapeDtypeStruct((HALF, ROWS), F32),
        ],
        in_specs=[pl.BlockSpec(memory_space=pltpu.SMEM)] + [any_] * 6,
        out_specs=[any_] * 3,
        scratch_shapes=[
            pltpu.VMEM((TOK, D), BF16),
            pltpu.VMEM((1, D), F32),
            pltpu.VMEM((TOK, X), BF16),
            pltpu.VMEM((ROWS, X), BF16),
            pltpu.VMEM((2, HALF, ROWS), F32),
            pltpu.VMEM((2, HALF, ROWS), F32),
            pltpu.VMEM((TOK, 128), F32),
            pltpu.VMEM((15, TOK, ROWS), BF16),
            pltpu.VMEM((8, 2, TOK, ROWS), BF16),
            pltpu.VMEM((8, 2, X, TOK), BF16),
            pltpu.VMEM((RING, 2, HALF, ROWS), BF16),
            pltpu.VMEM((RING, HALF, ROWS), BF16),
            pltpu.VMEM((2, RING, HALF, ROWS), BF16),
            pltpu.VMEM((4, 2, HALF, ROWS), BF16),
            pltpu.VMEM((15, 2, HALF, ROWS), BF16),
            pltpu.VMEM((RING, 2, 2, HALF, ROWS), BF16),
            pltpu.VMEM((X, ROWS), F32),
            pltpu.VMEM((ROWS, X), BF16),
            pltpu.VMEM((2, HALF, ROWS), F32),
            pltpu.VMEM((2, HALF, ROWS), F32),
            dma((6,)), dma((10,)), dma((15,)), dma((15,)), dma((17,)), dma((17,)), dma((16,)), dma((2, 16)),
            dma((5,)), dma((5,)), dma((15,)), dma((15,)), dma((16,)), dma((16,)),
            dma((2, 17)), dma((17,)), dma((17,)), dma((17,)), pltpu.SemaphoreType.REGULAR,
        ],
        compiler_params=pltpu.CompilerParams(
            collective_id=0, has_side_effects=True, vmem_limit_bytes=60 << 20
        ),
        name="outer_sync",
    )(
        sync_step, hidden[0], norm_gain.reshape(1, D), dkeys[0], local_weights[0],
        outer_params.T, momentum.T,
    )
    results = [merged, outer_new, mom_new]
    merged, outer_new, mom_new = pl.pallas_call(
        copy_kernel,
        out_shape=[jax.ShapeDtypeStruct(a.shape, a.dtype) for a in results],
        in_specs=[any_] * 3,
        out_specs=[any_] * 3,
        scratch_shapes=[pltpu.VMEM(a.shape, a.dtype) for a in results] + [dma((6,)), dma((6,))],
        compiler_params=pltpu.CompilerParams(vmem_limit_bytes=60 << 20),
        name="results",
    )(*results)
    return merged[None], outer_new.T, mom_new.T


def solution(mesh):
    placed = (
        P("replica", "fsdp", None),
        P(),
        P("replica", "fsdp", None),
        P("replica", "fsdp", None),
        P("fsdp", "replica"),
        P("fsdp", "replica"),
        P(),
    )
    return jax.shard_map(
        on_device,
        mesh=mesh,
        in_specs=placed,
        out_specs=(P("replica", "fsdp", None), P("fsdp", "replica"), P("fsdp", "replica")),
        check_vma=False,
    )
```

time: 75.7 us -> 70.1 us (0.926)
  the two profiles are of different devices: /device:TPU:4 before, /device:TPU:1 now
where the time goes in v3:
time: 70.1 us; the launch traced here: 69.9 us
  Pallas kernels  68.6 us (98%)
  between operations  1.29 us (2%)
    pallas_call x1, Pallas kernels, on_device(): pl.pallas_call(kernel, out_shape=[jax.ShapeDtypeStruct((ROWS, X), BF16),...  66.6 us
    pallas_call x1, Pallas kernels, on_device(): pl.pallas_call(copy_kernel, out_shape=[jax.ShapeDtypeStruct(a.shape, a.dt...  2.05 us

profile of v3, /device:TPU:1, one launch (start us, length us, event | category | flops | bytes accessed | tf_op | source)
XLA Modules:
  0.0 69.9 jit_solution(15888481299047790928)
XLA Ops:
  1.3 66.6 %outer_sync.1 = (bf16[512,1024]{1,0:T(8,128)(2,1)}, f32[32,512]{1,0:T(8,128)}, f32[32,512]{1,0:T(8,128)}) custom-call(s32[1]{0:T(128)S(6)} %copy.10.step, bf16[128,8192]{1,0:T(8,128)(2,1)} %bitcast.9, f32[1,8192]{1,0:T(1,128)} %bitcast.14, bf16[128,1024]{1,0:T(8,128)(2,1)} %bitcast.11, bf16[512,1024]{1,0:T(8,128)(2,1)} %bitcast.10, f32[32,512]{1,0:T(8,128)} %bitcast.12, ...), custom_call_target="tpu_custom_call" | custom-call | tf_op jit(solution)/shard_map/outer_sync/pallas_call | solution.py:411
  67.9 2.1 %results.1 = (bf16[512,1024]{1,0:T(8,128)(2,1)}, f32[32,512]{1,0:T(8,128)}, f32[32,512]{1,0:T(8,128)}) custom-call(bf16[512,1024]{1,0:T(8,128)(2,1)} %get-tuple-element.9.merged, f32[32,512]{1,0:T(8,128)} %get-tuple-element.10.outer_new, f32[32,512]{1,0:T(8,128)} %get-tuple-element.11.mom_new), custom_call_target="tpu_custom_call" | custom-call | tf_op jit(solution)/shard_map/results/pallas_call | solution.py:454

commit v4 on v3

--- a/solution.py
+++ b/solution.py
@@ -362,13 +362,13 @@
         pair_send(partner)
         keys_own()
         statistics()
-        a2a_send(0, 4)
         arrive(other_wt, core_r.at[0])
+        a2a_send(0, 2)
         neighbours_are_in()
         rs_step(0)
-        a2a_send(4, 10)
+        a2a_send(2, 7)
         rs_step(1)
-        a2a_send(10, 15)
+        a2a_send(7, 15)
         own_block()
         rs_step(2)
         rs_step(3)

time: 70.1 us -> 68.7 us (0.980)
  Pallas kernels: 68.6 us -> 67.3 us
    pallas_call x1, Pallas kernels: 66.6 us -> 65.2 us  [on_device(): pl.pallas_call(kernel, out_shape=[jax.ShapeDtypeStruct((ROWS, X), BF16),...]
where the time goes in v4:
time: 68.7 us; the launch traced here: 68.6 us
  Pallas kernels  67.3 us (98%)
  between operations  1.29 us (2%)
    pallas_call x1, Pallas kernels, on_device(): pl.pallas_call(kernel, out_shape=[jax.ShapeDtypeStruct((ROWS, X), BF16),...  65.2 us
    pallas_call x1, Pallas kernels, on_device(): pl.pallas_call(copy_kernel, out_shape=[jax.ShapeDtypeStruct(a.shape, a.dt...  2.05 us

profile of v4, /device:TPU:1, one launch (start us, length us, event | category | flops | bytes accessed | tf_op | source)
XLA Modules:
  0.0 68.6 jit_solution(16660909865563078955)
XLA Ops:
  1.3 65.2 %outer_sync.1 = (bf16[512,1024]{1,0:T(8,128)(2,1)}, f32[32,512]{1,0:T(8,128)}, f32[32,512]{1,0:T(8,128)}) custom-call(s32[1]{0:T(128)S(6)} %copy.10.step, bf16[128,8192]{1,0:T(8,128)(2,1)} %bitcast.9, f32[1,8192]{1,0:T(1,128)} %bitcast.14, bf16[128,1024]{1,0:T(8,128)(2,1)} %bitcast.11, bf16[512,1024]{1,0:T(8,128)(2,1)} %bitcast.10, f32[32,512]{1,0:T(8,128)} %bitcast.12, ...), custom_call_target="tpu_custom_call" | custom-call | tf_op jit(solution)/shard_map/outer_sync/pallas_call | solution.py:411
  66.5 2.1 %results.1 = (bf16[512,1024]{1,0:T(8,128)(2,1)}, f32[32,512]{1,0:T(8,128)}, f32[32,512]{1,0:T(8,128)}) custom-call(bf16[512,1024]{1,0:T(8,128)(2,1)} %get-tuple-element.9.merged, f32[32,512]{1,0:T(8,128)} %get-tuple-element.10.outer_new, f32[32,512]{1,0:T(8,128)} %get-tuple-element.11.mom_new), custom_call_target="tpu_custom_call" | custom-call | tf_op jit(solution)/shard_map/results/pallas_call | solution.py:454
